TPU v7x, 32 devices: a whole 2x2x4 slice. The times are simulated.
32 devices in a mesh: blk: 8 (over z, x), dp: 4 (over y, core).
Axes of the slice: x: 2, y: 2, z: 4, core: 2. Of those that a mesh axis runs over, the one named last changes fastest.
Arguments:
- tokens: bfloat16 [4, 1024, 1472], P('dp', 'blk'), may hold values from -6 to 6
- lengths: int32 [4, 8], P('dp'), may hold values from 1 to 1024, as said below
- bucket_table: int32 [257], replicated, may hold values from 0 to 31
- first_gain: bfloat16 [1472], replicated, may hold values from 0.5 to 1.5
- position_bias: bfloat16 [32, 6], replicated, may hold values from -4 to 4
- w_query: bfloat16 [1472, 384], replicated, may hold values from -0.02734375 to 0.02734375
- w_key: bfloat16 [1472, 384], replicated, may hold values from -0.15625 to 0.15625
- w_value: bfloat16 [1472, 384], replicated, may hold values from -0.15625 to 0.15625
- w_output: bfloat16 [384, 1472], replicated, may hold values from -3 to 3
- second_gain: bfloat16 [1472], replicated, may hold values from 0.5 to 1.5
- w_gate: bfloat16 [1472, 3584], replicated, may hold values from -0.15625 to 0.15625
- w_up: bfloat16 [1472, 3584], replicated, may hold values from -0.15625 to 0.15625
- w_down: bfloat16 [3584, 1472], replicated, may hold values from -0.1875 to 0.1875
- cotangent: bfloat16 [4, 1024, 1472], P('dp', 'blk'), may hold values from -6 to 6
Outputs:
- mixed: bfloat16 [4, 1024, 1472], P('dp', 'blk')
- tokens_gradient: float32 [4, 1024, 1472], P('dp', 'blk')
- first_gain_gradient: float32 [1472], replicated
- position_bias_gradient: float32 [32, 6], replicated
- query_gradient: float32 [1472, 384], P(None, 'blk')
- key_gradient: float32 [1472, 384], P(None, 'blk')
- value_gradient: float32 [1472, 384], P(None, 'blk')
- output_gradient: float32 [384, 1472], P('blk')
- second_gain_gradient: float32 [1472], replicated
- gate_gradient: float32 [1472, 3584], P(None, ('blk', 'dp'))
- up_gradient: float32 [1472, 3584], P(None, ('blk', 'dp'))
- down_gradient: float32 [3584, 1472], P(('blk', 'dp'))
Inputs may be any that keep to these rules, and one draw needn't show every extreme that they name: `lengths`: each row sums to 1024; in each row one item, at a place drawn from the seed, begins within the first 128 positions and ends within the last 128; every other item is at most 16 long.
All inputs are finite; a program needn't handle non-finite values.
Results may differ from a plain program's by a relative error of at most 0.023.
Values may be sent and summed in bfloat16 or wider, within the bound.
A program may use at most 256 MiB of HBM per device.

v0:
```python
import math

import jax
import jax.numpy as jnp
from jax import lax
from jax.sharding import PartitionSpec as P


def normalize(values, gain):
    return values * lax.rsqrt(jnp.mean(values * values, axis=-1, keepdims=True) + 1e-06) * gain


def gelu_tanh(values):
    return (
        0.5
        * values
        * (
            1.0
            + jnp.tanh(math.sqrt(2.0 / math.pi) * (values + 0.044715 * values * values * values))
        )
    )


def activate(gate, up_part):
    return gelu_tanh(gate) * up_part


def blocked(block_fn, carry, piece):
    count = piece[0].shape[0]
    size = 512
    parts = tuple((arr.reshape((count // size, size) + arr.shape[1:]) for arr in piece))

    def visit(state, inputs):
        number, block = inputs
        return (block_fn(state, block, number * size), None)

    state, _ = lax.scan(visit, carry, (jnp.arange(count // size, dtype=jnp.int32), parts))
    return state


def diagonal_sums(slope, shift, reach, table_len):
    heads, rows, cols = slope.shape
    width = rows + cols
    flipped = slope[:, ::-1, :]
    padded = jnp.pad(flipped, ((0, 0), (0, 0), (0, rows)))
    skewed = padded.reshape(heads, rows * width)[:, : rows * (width - 1)].reshape(
        heads, rows, width - 1
    )
    diagonal = jnp.sum(skewed, axis=1)
    relative = shift + jnp.arange(width - 1, dtype=jnp.int32) - (rows - 1)
    index = jnp.clip(relative, -reach, reach) + reach
    selector = (index[:, None] == jnp.arange(table_len, dtype=jnp.int32)[None, :]).astype(
        jnp.float32
    )
    return jnp.dot(
        diagonal, selector, precision=lax.Precision.HIGHEST, preferred_element_type=jnp.float32
    )


def on_device(
    tokens,
    lengths,
    bucket_table,
    first_gain,
    position_bias,
    w_query,
    w_key,
    w_value,
    w_output,
    second_gain,
    w_gate,
    w_up,
    w_down,
    cotangent,
):
    f32 = jnp.float32
    bf16 = jnp.bfloat16
    heads = position_bias.shape[1]
    inner = w_query.shape[1]
    head_size = inner // heads
    local = tokens.shape[1]
    table_len = bucket_table.shape[0]
    reach = (table_len - 1) // 2
    inputs = tokens[0].astype(f32)
    positions = lax.axis_index("blk") * local + jnp.arange(local, dtype=jnp.int32)
    ends = jnp.cumsum(lengths[0])
    onehot = (
        bucket_table[:, None] == jnp.arange(position_bias.shape[0], dtype=jnp.int32)[None, :]
    ).astype(f32)
    head_rows = jnp.einsum(
        "rb,bh->hr", onehot, position_bias.astype(f32), precision=lax.Precision.HIGHEST
    )

    def item_of(places):
        return jnp.sum((places[:, None] >= ends[None, :]).astype(jnp.int32), axis=1)

    def pair_scores(query3, key3, query_pos, key_pos):
        offset = jnp.clip(key_pos[None, :] - query_pos[:, None], -reach, reach) + reach
        raw = jnp.einsum("qhd,khd->hqk", query3, key3, preferred_element_type=f32) + jnp.take(
            head_rows, offset, axis=1
        )
        mask = item_of(query_pos)[:, None] == item_of(key_pos)[None, :]
        return (jnp.where(mask[None], raw, -1e30), mask)

    normed_first, first_back = jax.vjp(normalize, inputs, first_gain.astype(f32))
    normed_first_low = normed_first.astype(bf16)
    queries = jnp.dot(normed_first_low, w_query, preferred_element_type=f32).astype(bf16)
    keys_low = jnp.dot(normed_first_low, w_key, preferred_element_type=f32).astype(bf16)
    values_low = jnp.dot(normed_first_low, w_value, preferred_element_type=f32).astype(bf16)
    query3 = queries.reshape(local, heads, head_size)
    key3_own = keys_low.reshape(local, heads, head_size)
    value3_own = values_low.reshape(local, heads, head_size)

    def forward_block(state, piece, start):
        high, total, running = state
        key_piece, value_piece = piece
        count = key_piece.shape[0]
        key_pos = start + jnp.arange(count, dtype=jnp.int32)
        scores, mask = pair_scores(
            query3, key_piece.reshape(count, heads, head_size), positions, key_pos
        )
        new_high = jnp.maximum(high, jnp.max(scores, axis=-1))
        weights = jnp.where(mask[None], jnp.exp(scores - new_high[..., None]), 0.0)
        factor = jnp.exp(high - new_high)
        total = total * factor + jnp.sum(weights, axis=-1)
        running = running * factor.T[:, :, None] + jnp.einsum(
            "hqk,khd->qhd",
            weights.astype(bf16),
            value_piece.reshape(count, heads, head_size),
            preferred_element_type=f32,
        )
        return (new_high, total, running)

    start_state = (
        jnp.full((heads, local), -1e30, f32),
        jnp.zeros((heads, local), f32),
        jnp.zeros((local, heads, head_size), f32),
    )
    high, total, running = blocked(
        forward_block,
        start_state,
        (
            lax.all_gather(keys_low, "blk", axis=0, tiled=True),
            lax.all_gather(values_low, "blk", axis=0, tiled=True),
        ),
    )
    log_total = high + jnp.log(total)
    attended = running / total.T[:, :, None]
    attention = attended.reshape(local, inner).astype(bf16)
    middle = inputs + jnp.dot(attention, w_output, preferred_element_type=f32)
    normed_second, second_back = jax.vjp(normalize, middle, second_gain.astype(f32))
    normed_second_low = normed_second.astype(bf16)
    gate = jnp.dot(normed_second_low, w_gate, preferred_element_type=f32)
    up_part = jnp.dot(normed_second_low, w_up, preferred_element_type=f32)
    hidden, activate_back = jax.vjp(activate, gate, up_part)
    hidden_low = hidden.astype(bf16)
    mixed = (middle + jnp.dot(hidden_low, w_down, preferred_element_type=f32)).astype(bf16)
    upstream = cotangent[0]
    down_local = jnp.einsum("td,tf->df", upstream, hidden_low, preferred_element_type=f32)
    hidden_slope = jnp.einsum("td,fd->tf", upstream, w_down, preferred_element_type=f32)
    gate_raw, up_raw = activate_back(hidden_slope)
    gate_slope = gate_raw.astype(bf16)
    up_slope = up_raw.astype(bf16)
    gate_local = jnp.einsum("td,tf->df", normed_second_low, gate_slope, preferred_element_type=f32)
    up_local = jnp.einsum("td,tf->df", normed_second_low, up_slope, preferred_element_type=f32)
    second_slope = jnp.einsum(
        "tf,df->td", gate_slope, w_gate, preferred_element_type=f32
    ) + jnp.einsum("tf,df->td", up_slope, w_up, preferred_element_type=f32)
    middle_norm_slope, second_gain_local = second_back(second_slope)
    middle_slope = upstream.astype(f32) + middle_norm_slope
    feed_parts = None
    branch_slope = middle_slope.astype(bf16)
    output_local = jnp.einsum("td,ti->di", branch_slope, attention, preferred_element_type=f32)
    attention_slope = jnp.einsum(
        "td,id->ti", branch_slope, w_output, preferred_element_type=f32
    ).astype(bf16)
    slope3 = attention_slope.reshape(local, heads, head_size)
    delta_rows = jnp.sum(slope3.astype(f32) * attended, axis=-1)
    delta_heads = delta_rows.T

    def query_block(state, piece, start):
        query_acc, table_acc = state
        key_piece, value_piece = piece
        count = key_piece.shape[0]
        key_pos = start + jnp.arange(count, dtype=jnp.int32)
        key3 = key_piece.reshape(count, heads, head_size)
        scores, mask = pair_scores(query3, key3, positions, key_pos)
        weights = jnp.where(mask[None], jnp.exp(scores - log_total[..., None]), 0.0)
        value_dots = jnp.einsum(
            "qhd,khd->hqk",
            slope3,
            value_piece.reshape(count, heads, head_size),
            preferred_element_type=f32,
        )
        score_slope = (weights * (value_dots - delta_heads[..., None])).astype(bf16)
        query_acc = query_acc + jnp.einsum(
            "hqk,khd->qhd", score_slope, key3, preferred_element_type=f32
        )
        table_acc = table_acc + diagonal_sums(
            score_slope.astype(f32), start - positions[0], reach, table_len
        )
        return (query_acc, table_acc)

    query_init = (jnp.zeros((local, heads, head_size), f32), jnp.zeros((heads, table_len), f32))
    query_acc, table_acc = blocked(
        query_block,
        query_init,
        (
            lax.all_gather(keys_low, "blk", axis=0, tiled=True),
            lax.all_gather(values_low, "blk", axis=0, tiled=True),
        ),
    )
    whole_total, whole_delta = (
        lax.all_gather(log_total.T, "blk", axis=0, tiled=True),
        lax.all_gather(delta_rows, "blk", axis=0, tiled=True),
    )

    def key_block(state, piece, start):
        key_acc, value_acc = state
        query_piece, slope_piece = piece
        count = query_piece.shape[0]
        query_pos = start + jnp.arange(count, dtype=jnp.int32)
        query3p = query_piece.reshape(count, heads, head_size)
        slope3p = slope_piece.reshape(count, heads, head_size)
        scores, mask = pair_scores(query3p, key3_own, query_pos, positions)
        piece_total = lax.dynamic_slice_in_dim(whole_total, start, count, 0).T
        piece_delta = lax.dynamic_slice_in_dim(whole_delta, start, count, 0).T
        weights = jnp.where(mask[None], jnp.exp(scores - piece_total[..., None]), 0.0)
        value_dots = jnp.einsum("qhd,khd->hqk", slope3p, value3_own, preferred_element_type=f32)
        score_slope = (weights * (value_dots - piece_delta[..., None])).astype(bf16)
        key_acc = key_acc + jnp.einsum(
            "hqk,qhd->khd", score_slope, query3p, preferred_element_type=f32
        )
        value_acc = value_acc + jnp.einsum(
            "hqk,qhd->khd", weights.astype(bf16), slope3p, preferred_element_type=f32
        )
        return (key_acc, value_acc)

    key_init = (
        jnp.zeros((local, heads, head_size), f32),
        jnp.zeros((local, heads, head_size), f32),
    )
    key_acc, value_acc = blocked(
        key_block,
        key_init,
        (
            lax.all_gather(queries, "blk", axis=0, tiled=True),
            lax.all_gather(attention_slope, "blk", axis=0, tiled=True),
        ),
    )
    query_slope = query_acc.reshape(local, inner).astype(bf16)
    key_slope = key_acc.reshape(local, inner).astype(bf16)
    value_slope = value_acc.reshape(local, inner).astype(bf16)
    query_local = jnp.einsum("td,ti->di", normed_first_low, query_slope, preferred_element_type=f32)
    key_local = jnp.einsum("td,ti->di", normed_first_low, key_slope, preferred_element_type=f32)
    value_local = jnp.einsum("td,ti->di", normed_first_low, value_slope, preferred_element_type=f32)
    first_slope = (
        jnp.einsum("ti,di->td", query_slope, w_query, preferred_element_type=f32)
        + jnp.einsum("ti,di->td", key_slope, w_key, preferred_element_type=f32)
        + jnp.einsum("ti,di->td", value_slope, w_value, preferred_element_type=f32)
    )
    input_norm_slope, first_gain_local = first_back(first_slope)
    tokens_gradient = middle_slope + input_norm_slope
    bias_local = jnp.einsum("rb,hr->bh", onehot, table_acc, precision=lax.Precision.HIGHEST)
    feed_parts = (
        lax.psum_scatter(gate_local, ("blk", "dp"), scatter_dimension=1, tiled=True),
        lax.psum_scatter(up_local, ("blk", "dp"), scatter_dimension=1, tiled=True),
        lax.psum_scatter(down_local, ("blk", "dp"), scatter_dimension=1, tiled=True),
    )
    attention_parts = (
        lax.psum_scatter(
            query_local.astype(jnp.bfloat16), "blk", scatter_dimension=1, tiled=True
        ).astype(jnp.float32),
        lax.psum_scatter(
            key_local.astype(jnp.bfloat16), "blk", scatter_dimension=1, tiled=True
        ).astype(jnp.float32),
        lax.psum_scatter(
            value_local.astype(jnp.bfloat16), "blk", scatter_dimension=1, tiled=True
        ).astype(jnp.float32),
        lax.psum_scatter(
            output_local.astype(jnp.bfloat16), "blk", scatter_dimension=1, tiled=True
        ).astype(jnp.float32),
    )
    attention_parts = (
        lax.psum(attention_parts[0].astype(jnp.bfloat16), "dp").astype(jnp.float32),
        lax.psum(attention_parts[1].astype(jnp.bfloat16), "dp").astype(jnp.float32),
        lax.psum(attention_parts[2].astype(jnp.bfloat16), "dp").astype(jnp.float32),
        lax.psum(attention_parts[3].astype(jnp.bfloat16), "dp").astype(jnp.float32),
    )
    first_total, bias_total, second_total = lax.psum(
        (first_gain_local, bias_local, second_gain_local), ("blk", "dp")
    )
    return (
        mixed[None],
        tokens_gradient[None],
        first_total,
        bias_total,
        attention_parts[0],
        attention_parts[1],
        attention_parts[2],
        attention_parts[3].T,
        second_total,
        feed_parts[0],
        feed_parts[1],
        feed_parts[2].T,
    )


def solution(mesh):
    return jax.shard_map(
        on_device,
        mesh=mesh,
        in_specs=(
            P("dp", "blk", None),
            P("dp", None),
            P(),
            P(),
            P(),
            P(),
            P(),
            P(),
            P(),
            P(),
            P(),
            P(),
            P(),
            P("dp", "blk", None),
        ),
        out_specs=(
            P("dp", "blk", None),
            P("dp", "blk", None),
            P(),
            P(),
            P(None, "blk"),
            P(None, "blk"),
            P(None, "blk"),
            P("blk", None),
            P(),
            P(None, ("blk", "dp")),
            P(None, ("blk", "dp")),
            P(("blk", "dp"), None),
        ),
        check_vma=False,
    )
```

profile of v0, /device:TPU:1, one launch (start us, length us, event | category | flops | bytes accessed | tf_op | source)
XLA Modules:
  0.0 2661.9 jit_solution(1661541368840575239)
XLA Ops:
  13.1 30.0 %all_gather.20 = bf16[1024,384]{1,0:T(8,128)(2,1)} all-gather(bf16[128,384]{1,0:T(8,128)(2,1)S(1)} %convolution_convert_fusion.7), channel_id=1, replica_groups=mesh['blk'=8,'dp'=4] {'blk'}, dimensions={0}, use_global_device_ids=true | all-gather | bytes 884736 | tf_op jit(solution)/shard_map/all_gather | solution.py:143
  48.1 26.6 all_gather.21
  75.9 483.1 %while.45 = (s32[]{:T(128)}, f32[6,128]{1,0:T(8,128)S(1)}, f32[6,128]{1,0:T(8,128)S(1)}, f32[128,6,64]{0,2,1:T(8,128)S(1)}, s32[8]{0:T(128)S(1)}, /*index=5*/s32...) while((s32[]{:T(128)}, f32[6,128]{1,0:T(8,128)S(1)}, ...), condition=%wide.region_7.9_spmd.clone, body=%wide.region_2.8_spmd.clone.sunk | while | flops 105876992 | bytes 24149296 | solution.py:37
  77.5 215.9 %gather_fusion = f32[65536,6]{1,0:T(8,128)} fusion(f32[6,257]{0,1:T(8,128)S(1)} %get-tuple-element.1121, s32[65536]{0:T(1024)S(1)} %broadcast_clamp_fusion.4), kind=kCustom, calls=%fused_computation.clone.clone.1 | custom fusion | bytes 3407872 | tf_op jit(solution)/shard_map/while/body/eval_jaxpr/jit(_take)/gather | solution.py:99
  293.4 19.1 copy.145
  318.9 215.9 %gather_fusion = f32[65536,6]{1,0:T(8,128)} fusion(f32[6,257]{0,1:T(8,128)S(1)} %get-tuple-element.1121, s32[65536]{0:T(1024)S(1)} %broadcast_clamp_fusion.4), kind=kCustom, calls=%fused_computation.clone.clone.1 | custom fusion | bytes 3407872 | tf_op jit(solution)/shard_map/while/body/eval_jaxpr/jit(_take)/gather | solution.py:99
  588.0 526.0 %while.46 = (s32[]{:T(128)}, f32[128,6,64]{0,2,1:T(8,128)}, f32[6,257]{1,0:T(8,128)S(1)}, bf16[2,512,384]{1,2,0:T(8,128)(2,1)}, s32[128]{0:T(128)S(1)}, /*index=...) while((s32[]{:T(128)}, f32[128,6,64]{0,2,1:T(8,128)}, ...), condition=%wide.region_15.17_spmd.clone, body=%wide.region_11.16_spmd.clone.sunk | while | flops 167849152 | bytes 40751900 | solution.py:37
  590.9 215.9 %gather_fusion.1 = f32[65536,6]{1,0:T(8,128)} fusion(f32[6,257]{0,1:T(8,128)S(1)} %get-tuple-element.1169, s32[65536]{0:T(1024)S(1)} %broadcast_clamp_fusion.5), kind=kCustom, calls=%fused_computation.2.clone.clone.1 | custom fusion | bytes 3407872 | tf_op jit(solution)/shard_map/while/body/eval_jaxpr/jit(_take)/gather | solution.py:99
  853.4 215.9 %gather_fusion.1 = f32[65536,6]{1,0:T(8,128)} fusion(f32[6,257]{0,1:T(8,128)S(1)} %get-tuple-element.1169, s32[65536]{0:T(1024)S(1)} %broadcast_clamp_fusion.5), kind=kCustom, calls=%fused_computation.2.clone.clone.1 | custom fusion | bytes 3407872 | tf_op jit(solution)/shard_map/while/body/eval_jaxpr/jit(_take)/gather | solution.py:99
  1117.9 28.9 %all_gather.22 = bf16[1024,384]{1,0:T(8,128)(2,1)} all-gather(bf16[128,384]{1,0:T(8,128)(2,1)S(1)} %copy-done.28), channel_id=1, replica_groups=mesh['blk'=8,'dp'=4] {'blk'}, dimensions={0}, use_global_device_ids=true | all-gather | bytes 884736 | tf_op jit(solution)/shard_map/all_gather | solution.py:247
  1147.5 30.1 %all_gather.24 = bf16[1024,384]{1,0:T(8,128)(2,1)} all-gather(bf16[128,384]{1,0:T(8,128)(2,1)S(1)} %copy-done.32), channel_id=1, replica_groups=mesh['blk'=8,'dp'=4] {'blk'}, dimensions={0}, use_global_device_ids=true | all-gather | bytes 884736 | tf_op jit(solution)/shard_map/all_gather | solution.py:248
  1177.7 26.2 all_gather.25
  1204.0 25.3 all_gather.23
  1229.3 493.4 %while.47 = (s32[]{:T(128)}, f32[128,6,64]{0,2,1:T(8,128)S(1)}, f32[128,6,64]{0,2,1:T(8,128)}, bf16[2,512,384]{2,1,0:T(8,128)(2,1)}, s32[2]{0:T(128)S(1)}, /*ind...) while((s32[]{:T(128)}, f32[128,6,64]{0,2,1:T(8,128)S(1)}, ...), condition=%wide.region_19.21_spmd.clone, body=%wide.region_16.20_spmd.clone.sunk | while | flops 206191616 | bytes 20733388 | solution.py:37
  1233.4 215.9 %gather_fusion.2 = f32[65536,6]{1,0:T(8,128)} fusion(f32[6,257]{0,1:T(8,128)S(1)} %get-tuple-element.1219, s32[65536]{0:T(1024)S(1)} %fusion.209), kind=kCustom, calls=%fused_computation.1.clone.clone.1 | custom fusion | bytes 3407872 | tf_op jit(solution)/shard_map/while/body/eval_jaxpr/jit(_take)/gather | solution.py:99
  1479.4 215.9 %gather_fusion.2 = f32[65536,6]{1,0:T(8,128)} fusion(f32[6,257]{0,1:T(8,128)S(1)} %get-tuple-element.1219, s32[65536]{0:T(1024)S(1)} %fusion.209), kind=kCustom, calls=%fused_computation.1.clone.clone.1 | custom fusion | bytes 3407872 | tf_op jit(solution)/shard_map/while/body/eval_jaxpr/jit(_take)/gather | solution.py:99
  1728.9 93.0 %reduce-scatter.12.cloned.1.call-done = bf16[1472,48]{0,1:T(8,128)(2,1)} async-done(((bf16[1472,384]{0,1:T(8,128)(2,1)}), bf16[1472,48]{0,1:T(8,128)(2,1)}) %reduce-scatter.12.cloned.1.call-update) | async-done | bytes 141328 | tf_op jit(solution)/shard_map/reduce_scatter | solution.py:274
  1822.0 66.3 %reduce-scatter.14.cloned.1.call-done = bf16[1472,48]{0,1:T(8,128)(2,1)} async-done(((bf16[1472,384]{0,1:T(8,128)(2,1)}), bf16[1472,48]{0,1:T(8,128)(2,1)}) %reduce-scatter.14.cloned.1.call-update) | async-done | bytes 141328 | tf_op jit(solution)/shard_map/reduce_scatter | solution.py:277
  1888.2 66.4 %reduce-scatter.16.cloned.1.call-done = bf16[1472,48]{0,1:T(8,128)(2,1)} async-done(((bf16[1472,384]{0,1:T(8,128)(2,1)}), bf16[1472,48]{0,1:T(8,128)(2,1)}) %reduce-scatter.16.cloned.1.call-update) | async-done | bytes 141328 | tf_op jit(solution)/shard_map/reduce_scatter | solution.py:280
  1989.6 22.7 copy.124
  2016.9 45.7 %all-reduce.1 = (f32[1472]{0:T(1024)}, f32[32,6]{0,1:T(8,128)}, f32[1472]{0:T(1024)}) all-reduce(f32[1472]{0:T(1024)S(1)} %get-tuple-element.728, f32[32,6]{0,1:T(8,128)S(1)} %fusion.74, f32[1472]{0:T(1024)S(1)} %copy-done.38), channel_id=1, replica_groups=mesh['blk'=8,'dp'=4] {'blk','dp'}, use_global_device_ids=true, to_apply=%region_22.24 | all-reduce | flops 3136 | bytes 25088 | tf_op jit(solution)/shard_map/psum | solution.py:290
  2079.3 112.1 %reduce-scatter.18.cloned.1.call-done = f32[1472,112]{0,1:T(8,128)} async-done(((f32[1472,3584]{0,1:T(8,128)}), f32[1472,112]{0,1:T(8,128)}) %reduce-scatter.18.cloned.1.call-update) | async-done | bytes 659472 | tf_op jit(solution)/shard_map/reduce_scatter | solution.py:266
  2191.3 231.5 %reduce-scatter.20.cloned.1.call-done = f32[1472,112]{0,1:T(8,128)} async-done(((f32[1472,3584]{0,1:T(8,128)}), f32[1472,112]{0,1:T(8,128)}) %reduce-scatter.20.cloned.1.call-update) | async-done | bytes 659472 | tf_op jit(solution)/shard_map/reduce_scatter | solution.py:267
  2422.8 231.6 %reduce-scatter.22.cloned.1.call-done = f32[112,1472]{1,0:T(8,128)} async-done(((f32[3584,1472]{1,0:T(8,128)}), f32[112,1472]{1,0:T(8,128)}) %reduce-scatter.22.cloned.1.call-update) | async-done | bytes 659472 | tf_op jit(solution)/shard_map/transpose | solution.py:305
  (319 shorter events, 289.4 us)
Async XLA Ops:
  8.0 39.3 %copy-start = (bf16[1472,384]{1,0:T(8,128)(2,1)S(1)}, bf16[1472,384]{1,0:T(8,128)(2,1)}, u32[]{:S(2)}) copy-start(bf16[1472,384]{1,0:T(8,128)(2,1)} %param.29) | copy-start | bytes 3391492
  8.0 1720.9 %reduce-scatter.10.cloned.1.call-start = ((), (), s32[]{:S(2)}) async-start(), calls=%async_computation.7 | async-start | bytes 1327104 | tf_op jit(solution)/shard_map/reduce_scatter | solution.py:271
  9.7 37.6 %copy-start.33 = (f32[1472]{0:T(1024)}, f32[1472]{0:T(1024)S(1)}, u32[]{:S(2)}) copy-start(f32[1472]{0:T(1024)S(1)} %convert_element_type.186) | copy-start | bytes 17668
  10.9 34.5 %copy-start.40 = (f32[128]{0:T(128)}, f32[128]{0:T(128)S(1)}, u32[]{:S(2)}) copy-start(f32[128]{0:T(128)S(1)} %fusion.61) | copy-start | bytes 1540
  10.9 36.4 %copy-start.35 = (f32[128]{0:T(128)}, f32[128]{0:T(128)S(1)}, u32[]{:S(2)}) copy-start(f32[128]{0:T(128)S(1)} %fusion.78) | copy-start | bytes 1540
  13.1 33.1 %copy-start.23 = (bf16[128,384]{1,0:T(8,128)(2,1)}, bf16[128,384]{1,0:T(8,128)(2,1)S(1)}, u32[]{:S(2)}) copy-start(bf16[128,384]{1,0:T(8,128)(2,1)S(1)} %convolution_convert_fusion.7) | copy-start | bytes 294916
  75.9 483.1 %copy-start.39 = (bf16[1472]{0:T(1024)(128)(2,1)S(1)}, bf16[1472]{0:T(1024)(128)(2,1)}, u32[]{:S(2)}) copy-start(bf16[1472]{0:T(1024)(128)(2,1)} %param.31) | copy-start | bytes 8836
  588.0 527.1 %copy-start.34 = (f32[1472]{0:T(1024)S(1)}, f32[1472]{0:T(1024)}, u32[]{:S(2)}) copy-start(f32[1472]{0:T(1024)} %copy-done.33) | copy-start | bytes 17668
  588.0 527.1 %copy-start.36 = (f32[128]{0:T(128)S(1)}, f32[128]{0:T(128)}, u32[]{:S(2)}) copy-start(f32[128]{0:T(128)} %copy-done.35) | copy-start | bytes 1540
  1117.8 59.8 %copy-start.26 = (bf16[128,384]{1,0:T(8,128)(2,1)S(1)}, bf16[128,384]{1,0:T(8,128)(2,1)}, u32[]{:S(2)}) copy-start(bf16[128,384]{1,0:T(8,128)(2,1)} %copy-done.25) | copy-start | bytes 294916
  1117.8 704.1 %reduce-scatter.12.cloned.1.call-start = ((), (), s32[]{:S(2)}) async-start(), calls=%async_computation.8 | async-start | bytes 1327104 | tf_op jit(solution)/shard_map/reduce_scatter | solution.py:274
  1229.7 219.6 %copy-start.48 = (s32[2]{0:T(128)}, s32[2]{0:T(128)S(1)}, u32[]{:S(2)}) copy-start(s32[2]{0:T(128)S(1)} %get-tuple-element.1216) | copy-start | bytes 28 | tf_op jit(solution)/shard_map/while
  1231.9 237.5 %copy-start.2 = (bf16[1,512,384]{1,2,0:T(8,128)(2,1)}, bf16[1,512,384]{1,2,0:T(8,128)(2,1)S(1)}, u32[]{:S(2)}) copy-start(bf16[1,512,384]{1,2,0:T(8,128)(2,1)S(1)} %copy.152) | copy-start | bytes 1179652 | tf_op jit(solution)/shard_map/while
  1475.8 219.5 %copy-start.48 = (s32[2]{0:T(128)}, s32[2]{0:T(128)S(1)}, u32[]{:S(2)}) copy-start(s32[2]{0:T(128)S(1)} %get-tuple-element.1216) | copy-start | bytes 28 | tf_op jit(solution)/shard_map/while
  1477.9 237.5 %copy-start.2 = (bf16[1,512,384]{1,2,0:T(8,128)(2,1)}, bf16[1,512,384]{1,2,0:T(8,128)(2,1)S(1)}, u32[]{:S(2)}) copy-start(bf16[1,512,384]{1,2,0:T(8,128)(2,1)S(1)} %copy.152) | copy-start | bytes 1179652 | tf_op jit(solution)/shard_map/while
  1725.5 162.7 %reduce-scatter.14.cloned.1.call-start = ((), (), s32[]{:S(2)}) async-start(), calls=%async_computation.9 | async-start | bytes 1327104 | tf_op jit(solution)/shard_map/reduce_scatter | solution.py:277
  1727.2 227.4 %copy-start.8 = (bf16[128,1472]{0,1:T(8,128)(2,1)S(1)}, bf16[128,1472]{0,1:T(8,128)(2,1)}, u32[]{:S(2)}) copy-start(bf16[128,1472]{0,1:T(8,128)(2,1)} %copy-done.7) | copy-start | bytes 1130500
  1727.3 227.4 %reduce-scatter.16.cloned.1.call-start = ((), (), s32[]{:S(2)}) async-start(), calls=%async_computation.10 | async-start | bytes 1327104 | tf_op jit(solution)/shard_map/reduce_scatter | solution.py:280
  1728.9 343.8 %all-reduce.5.cloned.1.call-start = ((), (), s32[]{:S(2)}) async-start(), calls=%async_computation.14 | async-start | bytes 1179648 | tf_op jit(solution)/shard_map/psum | solution.py:285
  1954.6 236.7 %reduce-scatter.18.cloned.1.call-start = ((), (), s32[]{:S(2)}) async-start(), calls=%async_computation.11 | async-start | bytes 22708224 | tf_op jit(solution)/shard_map/reduce_scatter | solution.py:266
  1965.2 457.7 %reduce-scatter.20.cloned.1.call-start = ((), (), s32[]{:S(2)}) async-start(), calls=%async_computation.12 | async-start | bytes 22708224 | tf_op jit(solution)/shard_map/reduce_scatter | solution.py:267
  1976.7 677.7 %reduce-scatter.22.cloned.1.call-start = ((), (), s32[]{:S(2)}) async-start(), calls=%async_computation.13 | async-start | bytes 22708224 | tf_op jit(solution)/shard_map/transpose | solution.py:305
  2015.5 47.1 %copy-start.41 = (f32[128]{0:T(128)S(1)}, f32[128]{0:T(128)}, u32[]{:S(2)}) copy-start(f32[128]{0:T(128)} %copy-done.40) | copy-start | bytes 1540
  2016.9 48.1 %copy-start.6 = (f32[128,1472]{0,1:T(8,128)S(1)}, f32[128,1472]{0,1:T(8,128)}, u32[]{:S(2)}) copy-start(f32[128,1472]{0,1:T(8,128)} %copy-done.5) | copy-start | bytes 2260996
  (45 other events, 331.0 us)
Sparse Core Ops, SparseCore 0:
  1117.9 78.2 reduce-scatter.9
  1725.6 96.3 reduce-scatter.11
  1825.4 62.8 reduce-scatter.13
  1891.5 63.0 reduce-scatter.15
  1957.0 33.1 all-reduce.4
Sparse Core Ops, SparseCore 1:
  1965.3 226.0 reduce-scatter.17
  2198.2 224.6 reduce-scatter.19
  2429.7 224.6 reduce-scatter.21
where the time goes:
time: 2670 us; the launch traced here: 2660 us
  local copies, waits for them, and re-layouts  1490 us (56%)
  waiting for transfers between devices  801 us (30%)
  blocking collectives  213 us (8%)
  matrix products  113 us (4%)
    gather x12, local copies, waits for them, and re-layouts, pair_scores(): jnp.take(head_rows, offset, axis=1)  1410 us
    transpose x1, waiting for transfers between devices, on_device(): feed_parts[2]  232 us
    reduce_scatter x1, waiting for transfers between devices, on_device(): lax.psum_scatter(up_local, ('blk', 'dp'), scatter_dimension=1, tiled=True)  231 us
    reduce_scatter x1, waiting for transfers between devices, on_device(): lax.psum_scatter(gate_local, ('blk', 'dp'), scatter_dimension=1, tiled=True)  112 us
    reduce_scatter x1, waiting for transfers between devices, on_device(): lax.psum_scatter(key_local.astype(jnp.bfloat16), 'blk', scatter_dimension...  93 us
    reduce_scatter x1, waiting for transfers between devices, on_device(): lax.psum_scatter(output_local.astype(jnp.bfloat16), 'blk', scatter_dimens...  66.4 us
    reduce_scatter x1, waiting for transfers between devices, on_device(): lax.psum_scatter(value_local.astype(jnp.bfloat16), 'blk', scatter_dimensi...  66.3 us
  transfers between devices with their start and end apart: 8, of which 6 were waited for; matrix products, arithmetic and copies ran while one was open for 22% of the time, Pallas kernels for 0%

commit v1 on v0

--- a/solution.py
+++ b/solution.py
@@ -1,9 +1,1196 @@
+import functools
 import math
 
 import jax
 import jax.numpy as jnp
 from jax import lax
+from jax.experimental import pallas as pl
+from jax.experimental.pallas import tpu as pltpu
 from jax.sharding import PartitionSpec as P
+
+F32 = jnp.float32
+BF16 = jnp.bfloat16
+EPS = 1e-06
+ROOT = math.sqrt(2.0 / math.pi)
+HI = 4
+LANES = 128
+
+
+def nn(left, right):
+    return lax.dot_general(left, right, (((1,), (0,)), ((), ())), preferred_element_type=F32)
+
+
+def nt(left, right):
+    return lax.dot_general(left, right, (((1,), (1,)), ((), ())), preferred_element_type=F32)
+
+
+def tn(left, right):
+    return lax.dot_general(left, right, (((0,), (0,)), ((), ())), preferred_element_type=F32)
+
+
+def widen(value, lanes):
+    return jnp.concatenate(
+        [value, jnp.zeros((value.shape[0], lanes - value.shape[1]), value.dtype)], axis=1
+    )
+
+
+def activation(gate, up, hidden_slope):
+    square = gate * gate
+    bent = jnp.tanh(ROOT * gate * (1.0 + 0.044715 * square))
+    half = 0.5 * (1.0 + bent)
+    value = gate * half
+    slope = half + 0.5 * gate * (1.0 - bent * bent) * (ROOT * (1.0 + 3.0 * 0.044715 * square))
+    return (
+        (value * up).astype(BF16),
+        (hidden_slope * up * slope).astype(BF16),
+        (hidden_slope * value).astype(BF16),
+    )
+
+
+def layer_kernel(
+    n_blk,
+    n_dp,
+    lengths,
+    bucket_table,
+    first_gain,
+    second_gain,
+    bias_table,
+    tokens_hbm,
+    cot_hbm,
+    wq_hbm,
+    wk_hbm,
+    wv_hbm,
+    wo_hbm,
+    wg_hbm,
+    wu_hbm,
+    wd_hbm,
+    mixed_out,
+    tokgrad_out,
+    small_out,
+    attn_out,
+    ff_out,
+    tok_t,
+    cot_t,
+    tok,
+    wq,
+    wk,
+    wv,
+    wo,
+    k_all,
+    v_all,
+    q_all,
+    s_all,
+    totals,
+    deltas,
+    probs,
+    dq_rows,
+    gat,
+    streams,
+    held_w,
+    slopes,
+    middle,
+    mixed_acc,
+    second_acc,
+    attended,
+    swap_out,
+    swap_in,
+    ff_part,
+    ff_r1,
+    ff_r2,
+    rows,
+    acol,
+    grads_t,
+    at_part,
+    at_first,
+    at_recv,
+    ag,
+    small,
+    small_blk,
+    small_dp,
+    tables,
+    onehot,
+    diag,
+    lay,
+    load_sem,
+    stream_sem,
+    swap_sem,
+    k_send,
+    k_recv,
+    v_send,
+    v_recv,
+    q_send,
+    q_recv,
+    s_send,
+    s_recv,
+    lt_send,
+    lt_recv,
+    de_send,
+    de_recv,
+    gat_send,
+    gat_recv,
+    row_send,
+    row_recv,
+    col_send,
+    col_recv,
+    ff_send,
+    ff_sem,
+    at_send,
+    at_sem,
+    ag_send,
+    ag_sem,
+    sb_send,
+    sb_sem,
+    sd_send,
+    sd_sem,
+):
+    n_lo = n_blk // HI
+    local, width = tok.shape
+    lanes = rows.shape[2]
+    inner = wq.shape[1]
+    pairs = inner // LANES
+    heads = 2 * pairs
+    keys = n_blk * local
+    ff = wg_hbm.shape[1]
+    chunk = streams.shape[3]
+    slots = streams.shape[1]
+    half_ff = ff // 2
+    n_chunk = half_ff // chunk
+    cut = ff // (n_blk * n_dp)
+    n_near = HI // 2
+    last_dp = n_dp - 1
+
+    blk = lax.axis_index("blk")
+    dp = lax.axis_index("dp")
+    hi, lo = blk // n_lo, blk % n_lo
+    row_y, core = dp // 2, dp % 2
+    z_far, z_near = hi // 2, hi % 2
+    own = z_far * 4 + dp
+
+    def push(src, dst, send, recv, to_blk, to_dp):
+        return pltpu.make_async_remote_copy(
+            src_ref=src,
+            dst_ref=dst,
+            send_sem=send,
+            recv_sem=recv,
+            device_id={"blk": to_blk, "dp": to_dp},
+            device_id_type=pl.DeviceIdType.MESH,
+        )
+
+    loads = [
+        pltpu.make_async_copy(src, dst, load_sem.at[i])
+        for i, (src, dst) in enumerate(
+            (
+                (tokens_hbm, tok_t),
+                (wk_hbm, wk),
+                (wv_hbm, wv),
+                (wq_hbm, wq),
+                (cot_hbm, cot_t),
+                (wo_hbm, wo),
+            )
+        )
+    ]
+    for load in loads:
+        load.start()
+    feeds = (wg_hbm, wu_hbm, wd_hbm)
+    wide = chunk
+    picks = []
+    def piece_begin(q):
+        xl, zn = q // n_near, q % n_near
+        column = (((z_far * n_near + zn) * n_lo + xl) * n_dp + dp) * cut
+        return column, jnp.minimum(column // LANES * LANES, ff - wide)
+
+    for q in range(n_lo * n_near):
+        start = pl.multiple_of(piece_begin(q)[1], LANES)
+        for i, src in enumerate(feeds):
+            picks.append(
+                pltpu.make_async_copy(
+                    src.at[:, pl.ds(start, wide)], streams.at[i, q], stream_sem.at[i, q]
+                )
+            )
+    barrier = pltpu.get_barrier_semaphore()
+    partners = [((blk + o) % n_blk, dp) for o in range(1, n_blk)]
+    partners += [(blk, (dp + o) % n_dp) for o in range(1, n_dp)]
+    for to_blk, to_dp in partners:
+        pl.semaphore_signal(
+            barrier,
+            inc=1,
+            device_id={"blk": to_blk, "dp": to_dp},
+            device_id_type=pl.DeviceIdType.MESH,
+        )
+
+    z_other, near_other, lo_other = 1 - z_far, 1 - z_near, 1 - lo
+
+    def place(zf, zn, xl):
+        return (zf * n_near + zn) * n_lo + xl
+
+    class Gather:
+        def __init__(self, buf, send, recv):
+            self.buf, self.send, self.recv = buf, send, recv
+
+        def one(self, k, slot, to_blk):
+            ref = self.buf.at[slot]
+            return push(ref, ref, self.send.at[k], self.recv.at[k], to_blk, dp)
+
+        def far(self):
+            return self.one(0, blk, place(z_other, z_near, lo))
+
+        def near(self, a):
+            slot = place(z_other if a else z_far, z_near, lo)
+            return self.one(1 + a, slot, place(z_far, near_other, lo))
+
+        def low(self, a, b):
+            slot = place(z_other if a else z_far, near_other if b else z_near, lo)
+            return self.one(3 + 2 * a + b, slot, place(z_far, z_near, lo_other))
+
+        def start(self):
+            self.far().start()
+            self.near(0).start()
+            self.low(0, 0).start()
+
+        def step_near(self):
+            self.near(0).wait_recv()
+            self.low(0, 1).start()
+
+        def step_far(self):
+            self.far().wait_recv()
+            self.near(1).start()
+            self.low(1, 0).start()
+
+        def step_last(self):
+            self.near(1).wait_recv()
+            self.low(1, 1).start()
+
+        def finish(self):
+            for a in range(2):
+                for b in range(2):
+                    self.low(a, b).wait_recv()
+
+        def drain(self):
+            self.far().wait_send()
+            for a in range(2):
+                self.near(a).wait_send()
+                for b in range(2):
+                    self.low(a, b).wait_send()
+
+    k_ring = Gather(k_all, k_send, k_recv)
+    v_ring = Gather(v_all, v_send, v_recv)
+    q_ring = Gather(q_all, q_send, q_recv)
+    s_ring = Gather(s_all, s_send, s_recv)
+
+    eye = (
+        lax.broadcasted_iota(jnp.int32, (local, local), 0)
+        == lax.broadcasted_iota(jnp.int32, (local, local), 1)
+    ).astype(BF16)
+    gain1 = first_gain[...].astype(F32).reshape(1, width)
+    gain2 = second_gain[...].astype(F32).reshape(1, width)
+    loads[0].wait()
+    x = nt(eye, tok_t[...])
+    tok[...] = x.astype(BF16)
+    first_scale = lax.rsqrt(jnp.mean(x * x, axis=-1, keepdims=True) + EPS)
+    normed = (x * first_scale * gain1).astype(BF16)
+    rows[dp] = widen(normed, lanes)
+    loads[1].wait()
+    for load in picks:
+        load.start()
+    k_all[blk] = nn(normed, wk[...]).astype(BF16)
+    pl.semaphore_wait(barrier, len(partners))
+    k_ring.start()
+    loads[2].wait()
+    v_all[blk] = nn(normed, wv[...]).astype(BF16)
+    v_ring.start()
+
+    y_other, core_other = 1 - row_y, 1 - core
+
+    def row_push(k, slot, to, src=None):
+        src = rows.at[slot] if src is None else src
+        return push(src, rows.at[slot], row_send.at[k], row_recv.at[k], blk, to)
+
+    other_dp = row_y * 2 + core_other
+
+    def row_across():
+        return row_push(0, dp, other_dp)
+
+    def row_down():
+        return row_push(1, dp, core)
+
+    def row_on():
+        return row_push(2, 2 + core, core_other)
+
+    def row_up(src=None):
+        return row_push(3 + core, dp, 2, src)
+
+    def row_across_last():
+        return row_push(7, dp, last_dp, brow)
+
+    def row_last(src):
+        return row_push(5 + core, dp, last_dp, src)
+
+    lower = row_y == 0
+    last = dp == last_dp
+
+    def to_dp(o, who):
+        return (dp + o) % n_dp == who
+
+    pl.when(dp != 2)(lambda: row_across().start())
+    pl.when(jnp.logical_not(lower))(lambda: row_down().start())
+
+    loads[3].wait()
+    q_all[blk] = nn(normed, wq[...]).astype(BF16)
+    loads[4].wait()
+    gat[1, own] = widen(nt(eye, cot_t[...]).astype(BF16), lanes)
+
+
+    def gat_push(which, k, slot, to_blk, to_dp, at=slice(None)):
+        ref = gat.at[which, slot, at]
+        return push(ref, ref, gat_send.at[which, k], gat_recv.at[which, k], to_blk, to_dp)
+
+    parts = [pl.ds(0, local // 2), pl.ds(local // 2, local // 2)]
+
+    def gat_z(which, part):
+        to = (z_other * n_near + z_near) * n_lo + lo
+        return gat_push(which, part, own, to, dp, parts[part])
+
+    def gat_y(which):
+        return gat_push(which, 2, own, blk, y_other * 2 + core)
+
+    def gat_y_far(which, part):
+        slot = z_other * 4 + dp
+        return gat_push(which, 3 + part, slot, blk, y_other * 2 + core, parts[part])
+
+    def gat_core(which, a, b):
+        slot = (z_far + a) % 2 * 4 + (row_y + b) % 2 * 2 + core
+        return gat_push(which, 5 + a * 2 + b, slot, blk, row_y * 2 + core_other)
+
+    def gat_far(which):
+        for part in range(2):
+            gat_z(which, part).start()
+
+    def gat_start(which):
+        gat_y(which).start()
+        gat_core(which, 0, 0).start()
+
+    def gat_forward(which, part):
+        gat_z(which, part).wait_recv()
+        gat_y_far(which, part).start()
+        if part:
+            gat_core(which, 1, 0).start()
+
+    def gat_across(which, a):
+        if a:
+            for part in range(2):
+                gat_y_far(which, part).wait_recv()
+        else:
+            gat_y(which).wait_recv()
+        gat_core(which, a, 1).start()
+
+    gat_start(1)
+    r = lax.broadcasted_iota(jnp.int32, (cut, wide), 0)
+    c = lax.broadcasted_iota(jnp.int32, (cut, wide), 1)
+    for load in picks:
+        load.wait()
+    def pick_piece(k, carry):
+        q, i = k // 3, k % 3
+        column, start = piece_begin(q)
+        pick = jnp.where(c - r == column - start, 1.0, 0.0).astype(BF16)
+        piece = nt(pick, streams[i, q]).astype(BF16)
+        held_w[i, pl.ds(pl.multiple_of(q * cut, 16), cut), :] = widen(piece, lanes)
+        return carry
+
+    lax.fori_loop(0, 3 * n_lo * n_near, pick_piece, 0)
+
+    def stream(i, c):
+        begin = pl.multiple_of(core * half_ff + c * chunk, chunk)
+        slot = c % slots
+        return pltpu.make_async_copy(
+            feeds[i].at[:, pl.ds(begin, chunk)], streams.at[i, slot], stream_sem.at[i, slot]
+        )
+
+    def stream_next(i, c):
+        pl.when(c + slots < n_chunk)(lambda: stream(i, c + slots).start())
+
+    for c in range(slots):
+        for i in (2, 0, 1):
+            stream(i, c).start()
+    k_ring.step_near()
+    v_ring.step_near()
+
+    near_span = 4 * local
+    lane_near = lax.broadcasted_iota(jnp.int32, (8, near_span), 1)
+    n_table = bucket_table.shape[0]
+    n_bucket = bias_table.shape[1]
+    held_lanes = 3 * LANES
+    bucket = jnp.concatenate(
+        [
+            bucket_table[...].astype(F32).reshape(1, n_table),
+            jnp.zeros((1, held_lanes - n_table), F32),
+        ],
+        axis=1,
+    )
+    bucket = jnp.broadcast_to(bucket, (8, held_lanes))
+    turn = (
+        lax.broadcasted_iota(jnp.int32, (held_lanes, held_lanes), 0)
+        + lax.broadcasted_iota(jnp.int32, (held_lanes, held_lanes), 1)
+        == n_table - 1
+    ).astype(BF16)
+
+    def bias_rows(line):
+        line = jnp.concatenate([line, jnp.zeros((8, near_span - held_lanes), F32)], axis=1)
+        line = jnp.where(lane_near >= n_table, line[:, n_table - 1 : n_table], line)
+        moved = pltpu.roll(line, local - 1, 1)
+        moved = jnp.where(lane_near < local - 1, line[:, 0:1], moved)
+        hot = (
+            jnp.broadcast_to(moved[0:1], (n_bucket, near_span))
+            == lax.broadcasted_iota(jnp.int32, (n_bucket, near_span), 0).astype(F32)
+        ).astype(F32)
+        return hot, nn(bias_table[...], hot.astype(BF16))
+
+    hots, tables[0] = bias_rows(bucket)
+    onehot[...] = hots
+    tables[1] = bias_rows(nn(bucket.astype(BF16), turn))[1]
+    here_pos = blk * local + lax.broadcasted_iota(jnp.int32, (local, 1), 0)
+    pack_pos = lax.broadcasted_iota(jnp.int32, (1, keys), 1)
+    here_item = jnp.zeros((local, 1), jnp.int32)
+    pack_item = jnp.zeros((1, keys), jnp.int32)
+    end = jnp.int32(0)
+    for m in range(lengths.shape[1]):
+        end = end + lengths[0, m]
+        here_item += (here_pos >= end).astype(jnp.int32)
+        pack_item += (pack_pos >= end).astype(jnp.int32)
+
+    near_at = pl.multiple_of(blk * local, local)
+    inside = slice(local, local + keys)
+    lane_lay = lax.broadcasted_iota(jnp.int32, (1, lay.shape[1]), 1)
+
+    def bias_tile(turned, h):
+        line = tables[turned, pl.ds(h, 1), :]
+        ends_row = jnp.where(lane_lay < near_at, line[:, 0:1], line[:, near_span - 1 : near_span])
+        lay[...] = jnp.broadcast_to(ends_row, lay.shape)
+        rolled = pltpu.roll(
+            jnp.broadcast_to(line, (local, near_span)), 1, 1, stride=1, stride_axis=0
+        )
+        lay[:, pl.ds(near_at, 3 * local)] = rolled[:, local:]
+        return jnp.where(here_item == pack_item, lay[:, inside], -1e30)
+
+    def fill_bias(h, carry):
+        probs[h] = bias_tile(0, h)
+        return carry
+
+    lax.fori_loop(0, heads, fill_bias, 0)
+
+    k_ring.step_far()
+    gat_far(1)
+
+    both = pl.ds((z_far * n_near + row_y) * 2, 2)
+    gat_core(1, 0, 0).wait_recv()
+
+    def hidden_slopes(c, carry):
+        stream(2, c).wait()
+        rows_c = gat[1, both].reshape(2 * local, lanes)[:, 0:width]
+        slopes[c] = nn(rows_c, streams[2, c % slots]).astype(BF16)
+        stream_next(2, c)
+        return carry
+
+    third = n_chunk // 3
+    lax.fori_loop(0, third, hidden_slopes, 0)
+    k_ring.step_last()
+    v_ring.step_far()
+    lax.fori_loop(third, n_chunk, hidden_slopes, 0)
+    for c in range(slots):
+        stream(2, c).start()
+    k_ring.finish()
+
+    @pl.when(lower)
+    def _():
+        row_down().wait_recv()
+        row_on().start()
+
+    lane = lax.broadcasted_iota(jnp.int32, (local, LANES), 1)
+    low_half = lane < LANES // 2
+
+    def halves(block):
+        zero = jnp.zeros_like(block)
+        return jnp.concatenate(
+            [jnp.where(low_half, block, zero), jnp.where(low_half, zero, block)], axis=0
+        )
+
+    def joined(both):
+        return jnp.where(low_half, both[0:local], both[local:])
+
+    def pair_at(p):
+        return pl.ds(pl.multiple_of(p * LANES, LANES), LANES)
+
+    def cols_of(ref, p):
+        return ref[:, :, pair_at(p)].reshape(keys, LANES)
+
+    def softmax(p, stat):
+        raw = nt(halves(q_all[blk, :, pair_at(p)]), cols_of(k_all, p))
+        for s in range(2):
+            h = 2 * p + s
+            score = raw[s * local : (s + 1) * local] + probs[h]
+            high = jnp.max(score, axis=-1, keepdims=True)
+            expo = jnp.exp(score - high)
+            total = jnp.sum(expo, axis=-1, keepdims=True)
+            probs[h] = expo * (1.0 / total)
+            stat = jnp.where(lane == h, high + jnp.log(total), stat)
+        pl.when(p == 0)(v_ring.step_last)
+        return stat
+
+    stat = lax.fori_loop(0, pairs, softmax, jnp.zeros((local, LANES), F32))
+    mine_at = pl.ds(pl.multiple_of(blk * local, local), local)
+
+    def line_push(buf, send, recv, o):
+        mine = buf.at[:, mine_at]
+        return push(mine, mine, send.at[o], recv.at[o], (blk + o) % n_blk, dp)
+
+    def total_push(o):
+        return line_push(totals, lt_send, lt_recv, o)
+
+    def delta_push(o):
+        return line_push(deltas, de_send, de_recv, o)
+
+    q_ring.start()
+    totals[:, mine_at] = stat.T[0:8]
+    for o in range(1, n_blk):
+        total_push(o).start()
+    v_ring.finish()
+
+    def attend(p, carry):
+        low = probs[pl.ds(2 * p, 2)].reshape(2 * local, keys).astype(BF16)
+        attended[:, pair_at(p)] = joined(nn(low, cols_of(v_all, p)))
+        return carry
+
+    lax.fori_loop(0, pairs, attend, 0)
+
+    gat_forward(1, 0)
+    gat_forward(1, 1)
+    gat_across(1, 0)
+    loads[5].wait()
+    attention = attended[...].astype(BF16)
+    mid = tok[...].astype(F32) + nt(attention, wo[...])
+    middle[...] = mid
+    second_scale = lax.rsqrt(jnp.mean(mid * mid, axis=-1, keepdims=True) + EPS)
+    gat[0, own] = widen((mid * second_scale * gain2).astype(BF16), lanes)
+    gat_far(0)
+    gat_start(0)
+
+    grads_t[3] = attended[...].T.astype(BF16)
+
+    mixed_acc[...] = jnp.zeros_like(mixed_acc)
+    second_acc[...] = jnp.zeros_like(second_acc)
+    gat_core(0, 0, 0).wait_recv()
+
+    def feed(c, carry):
+        slot = c % slots
+        for i in range(3):
+            stream(i, c).wait()
+        normed2 = gat[0, both].reshape(2 * local, lanes)[:, 0:width]
+        gate = nn(normed2, streams[0, slot])
+        up = nn(normed2, streams[1, slot])
+        hidden, gate_slope, up_slope = activation(gate, up, slopes[c].astype(F32))
+        mixed_acc[...] += nt(hidden, streams[2, slot]).reshape(mixed_acc.shape)
+        total = nt(gate_slope, streams[0, slot]) + nt(up_slope, streams[1, slot])
+        second_acc[...] += total.reshape(second_acc.shape)
+        for i in range(3):
+            stream_next(i, c)
+        return carry
+
+    half = n_chunk // 2
+    lax.fori_loop(0, half, feed, 0)
+    q_ring.step_near()
+    q_ring.step_far()
+    gat_across(1, 1)
+    lax.fori_loop(half, n_chunk - 1, feed, 0)
+    gat_across(0, 0)
+    q_ring.step_last()
+    lax.fori_loop(n_chunk - 1, n_chunk, feed, 0)
+
+    def swap_push():
+        return push(swap_out, swap_in, swap_sem.at[0], swap_sem.at[1], blk, row_y * 2 + core_other)
+
+    swap_out[0] = widen(second_acc[core_other].astype(BF16), lanes)
+    swap_out[1] = widen(mixed_acc[core_other].astype(BF16), lanes)
+    swap_push().start()
+    gat_forward(0, 0)
+    swap_push().wait_recv()
+
+    mid = middle[...]
+    second_scale = lax.rsqrt(jnp.mean(mid * mid, axis=-1, keepdims=True) + EPS)
+    second_slope = second_acc[core] + swap_in[0, :, 0:width].astype(F32)
+    small[...] = jnp.zeros_like(small)
+    quarter = lanes // 4
+
+    def small_line(first_row, line):
+        line = widen(line, lanes)
+        for q in range(4):
+            at = slice(q * quarter, (q + 1) * quarter)
+            small[first_row + q : first_row + q + 1, 0:quarter] = line[:, at]
+
+    small_line(4, jnp.sum(second_slope * mid * second_scale, axis=0, keepdims=True))
+    scaled = second_slope * gain2
+    middle_slope = (
+        gat[1, own, :, 0:width].astype(F32)
+        + second_scale * scaled
+        - mid
+        * (second_scale * second_scale * second_scale)
+        * jnp.mean(scaled * mid, axis=-1, keepdims=True)
+    )
+    mixed_acc[core] = mid + mixed_acc[core] + swap_in[1, :, 0:width].astype(F32)
+    middle[...] = middle_slope
+    branch = middle_slope.astype(BF16)
+    s_all[blk] = nn(branch, wo[...]).astype(BF16)
+    s_ring.start()
+    product = s_all[blk].astype(F32) * attended[...]
+    delta_cols = jnp.zeros((local, LANES), F32)
+    for h in range(heads):
+        piece = product[:, (h // 2) * LANES : (h // 2 + 1) * LANES]
+        mine = low_half if h % 2 == 0 else jnp.logical_not(low_half)
+        delta = jnp.sum(jnp.where(mine, piece, 0.0), axis=-1, keepdims=True)
+        delta_cols = jnp.where(lane == h, delta, delta_cols)
+    deltas[:, mine_at] = delta_cols.T[0:8]
+    for o in range(1, n_blk):
+        delta_push(o).start()
+
+    swap_push().wait_send()
+    brow = swap_out.at[0]
+    brow[...] = widen(branch, lanes)
+
+    @pl.when(last)
+    def _():
+        row_across().wait_send()
+        row_down().wait_send()
+        rows[dp] = widen(branch, lanes)
+
+    def col_push(o):
+        to = (dp + o) % n_dp
+        begin = pl.multiple_of(dp * local, local)
+        return push(
+            grads_t.at[to],
+            acol.at[:, pl.ds(begin, local)],
+            col_send.at[o],
+            col_recv.at[o],
+            blk,
+            to,
+        )
+
+
+    step = 2 * local
+    held = held_w.shape[1]
+
+    def recompute(k, carry):
+        a, b = k // 2, k % 2
+
+        @pl.when(k > 0)
+        def _():
+            for which in range(2):
+                gat_core(which, a, b).wait_recv()
+
+        t = (z_far + a) % 2 * n_near + (row_y + b) % 2
+        rows_n = gat[0, pl.ds(2 * t, 2)].reshape(step, lanes)
+        rows_c = gat[1, pl.ds(2 * t, 2)].reshape(step, lanes)
+        gate = nt(held_w[0], rows_n)
+        up = nt(held_w[1], rows_n)
+        hidden_slope = nt(held_w[2], rows_c)
+        hidden, gate_slope, up_slope = activation(gate, up, hidden_slope)
+        streams[0, t, 0:held, :] = gate_slope
+        streams[1, t, 0:held, :] = up_slope
+        streams[2, t, 0:held, :] = hidden
+        return carry
+
+    lax.fori_loop(0, 1, recompute, 0)
+    gat_forward(0, 1)
+    s_ring.step_near()
+    pl.when(lower)(lambda: row_last(brow).start())
+    pl.when(dp == 2)(lambda: row_across_last().start())
+
+    flip = (
+        lax.broadcasted_iota(jnp.int32, (local, local), 0)
+        + lax.broadcasted_iota(jnp.int32, (local, local), 1)
+        == local - 1
+    ).astype(BF16)
+    diag[...] = jnp.zeros_like(diag)
+    lay[...] = jnp.zeros_like(lay)
+    def query_side(p, carry):
+        dots = nt(halves(s_all[blk, :, pair_at(p)]), cols_of(v_all, p))
+        ds = []
+        for s in range(2):
+            h = 2 * p + s
+            delta = jnp.sum(jnp.where(lane == h, delta_cols, 0.0), axis=-1, keepdims=True)
+            one = (probs[h] * (dots[s * local : (s + 1) * local] - delta)).astype(BF16)
+            wide_one = one.astype(F32)
+            lay[:, inside] = wide_one
+            near = lay[:, pl.ds(near_at, 3 * local)].astype(BF16)
+            padded = jnp.concatenate([nn(flip, near), jnp.zeros((local, local), F32)], axis=1)
+            skewed = pltpu.roll(padded, 0, 1, stride=1, stride_axis=0)
+            total = jnp.sum(wide_one, axis=0, keepdims=True)
+            before = jnp.sum(jnp.where(pack_pos < near_at - local, total, 0.0), axis=1, keepdims=True)
+            after = jnp.sum(
+                jnp.where(pack_pos >= near_at + 2 * local, total, 0.0), axis=1, keepdims=True
+            )
+            line = jnp.sum(skewed, axis=0, keepdims=True)
+            line = line + jnp.where(lane_near[0:1] == 0, before, 0.0)
+            diag[pl.ds(h, 1), :] = line + jnp.where(lane_near[0:1] == near_span - 1, after, 0.0)
+            ds.append(one)
+        dq = joined(nn(jnp.concatenate(ds, axis=0), cols_of(k_all, p)))
+        dq_rows[:, pair_at(p)] = dq.astype(BF16)
+        grads_t[0, pair_at(p), :] = dq.T.astype(BF16)
+        return carry
+
+    lax.fori_loop(0, pairs, query_side, 0)
+    for o in range(1, n_dp):
+        pl.when(jnp.logical_or(to_dp(o, 0), to_dp(o, last_dp)))(lambda o=o: col_push(o).start())
+    pl.when(lower)(lambda: row_up().start())
+    s_ring.step_far()
+    lax.fori_loop(1, 2, recompute, 0)
+
+    q_ring.finish()
+    for o in range(1, n_blk):
+        total_push(o).wait_recv()
+
+    def key_weights(p, carry):
+        raw = nt(halves(k_all[blk, :, pair_at(p)]), cols_of(q_all, p))
+        for s in range(2):
+            h = 2 * p + s
+            piece = slice(s * local, (s + 1) * local)
+            probs[h] = jnp.exp(raw[piece] + bias_tile(1, h) - totals[pl.ds(h, 1), :])
+        return carry
+
+    lax.fori_loop(0, pairs, key_weights, 0)
+
+    gat_across(0, 1)
+    s_ring.step_last()
+    lax.fori_loop(2, HI, recompute, 0)
+
+    lo_far, near_far = 1 - lo, 1 - z_near
+    along_lo_blk = hi * n_lo + lo_far
+    along_z_blk = (z_far * n_near + near_far) * n_lo + lo
+
+    def split():
+        return slice(0, 48), slice(48, cut)
+
+    def ff_hop(src, dst, w, k, to_blk):
+        return push(src, dst, ff_send.at[w, k], ff_sem.at[w, k], to_blk, dp)
+
+    def ff_hop1(w):
+        by_lo, by_z = split()
+        return (
+            ff_hop(ff_part.at[w, lo_far, :, by_lo], ff_r1.at[w, :, by_lo], w, 0, along_lo_blk),
+            ff_hop(ff_part.at[w, :, near_far, by_z], ff_r1.at[w, :, by_z], w, 1, along_z_blk),
+        )
+
+    def ff_hop2(w):
+        by_lo, by_z = split()
+        return (
+            ff_hop(ff_part.at[w, lo, near_far, by_lo], ff_r2.at[w, by_lo], w, 2, along_z_blk),
+            ff_hop(ff_part.at[w, lo_far, z_near, by_z], ff_r2.at[w, by_z], w, 3, along_lo_blk),
+        )
+
+    def ff_middle(w):
+        by_lo, by_z = split()
+        one, two = ff_hop1(w)
+        far, near = ff_hop2(w)
+        one.wait_recv()
+        ff_part[w, lo, near_far, by_lo] = (
+            ff_part[w, lo, near_far, by_lo].astype(F32) + ff_r1[w, near_far, by_lo].astype(F32)
+        ).astype(BF16)
+        far.start()
+        two.wait_recv()
+        ff_part[w, lo_far, z_near, by_z] = (
+            ff_part[w, lo_far, z_near, by_z].astype(F32) + ff_r1[w, lo_far, by_z].astype(F32)
+        ).astype(BF16)
+        near.start()
+
+    def ff_last(w):
+        by_lo, by_z = split()
+        far, near = ff_hop2(w)
+        far.wait_recv()
+        near.wait_recv()
+        mine = ff_part[w, lo, z_near].astype(F32) + ff_r2[w].astype(F32)
+        ff_out[w, by_lo] = mine[by_lo] + ff_r1[w, z_near, by_lo].astype(F32)
+        ff_out[w, by_z] = mine[by_z] + ff_r1[w, lo, by_z].astype(F32)
+
+    def at_hop1():
+        to = hi * n_lo + 1 - lo
+        return push(at_part.at[1 - lo], at_first, at_send.at[0], at_sem.at[0], to, dp)
+
+    def at_hop2(o):
+        to = (hi + o) % HI
+        return push(
+            at_part.at[lo, to], at_recv.at[hi], at_send.at[o], at_sem.at[o], to * n_lo + lo, dp
+        )
+
+    def attention_gradient():
+        acol[:, pl.ds(pl.multiple_of(dp * local, local), local)] = grads_t[dp]
+
+        @pl.when(lower)
+        def _():
+            row_across().wait_recv()
+            row_on().wait_recv()
+
+        @pl.when(dp == 2)
+        def _():
+            row_across().wait_recv()
+            for k in (3, 4):
+                row_push(k, dp, 2).wait_recv()
+
+        @pl.when(last)
+        def _():
+            for k in (5, 6, 7):
+                row_push(k, dp, last_dp).wait_recv()
+
+        for o in range(1, n_dp):
+            col_push(o).wait_recv()
+        total = nn(acol[...], rows[...].reshape(n_dp * local, lanes))
+        total = total.astype(BF16).reshape(n_blk, inner // n_blk, lanes)
+        for b in range(n_blk):
+            at_part[b % n_lo, b // n_lo] = total[b]
+        at_hop1().start()
+
+    def attention_gradient_next():
+        at_hop1().wait_recv()
+        at_part[lo] = (at_part[lo].astype(F32) + at_first[...].astype(F32)).astype(BF16)
+        for o in range(1, HI):
+            at_hop2(o).start()
+        at_recv[hi] = at_part[lo, hi]
+
+    early = jnp.logical_or(dp == 0, dp == last_dp)
+
+    order = (2, 0, 1)
+
+    def gradient(k, carry):
+        w = (k + 2) % 3
+        left = jnp.concatenate([streams[w, t, 0:held, :] for t in range(HI)], axis=1)
+        total = nn(left, gat[w // 2].reshape(2 * HI * local, lanes))
+        ff_part[w] = total.astype(BF16).reshape(n_lo, n_near, cut, lanes)
+        for hop in ff_hop1(w):
+            hop.start()
+        return carry
+
+    pl.when(early)(attention_gradient)
+    lax.fori_loop(0, 1, gradient, 0)
+
+    s_ring.finish()
+    for o in range(1, n_blk):
+        delta_push(o).wait_recv()
+
+    def key_side(p, carry):
+        queries = cols_of(q_all, p)
+        slopes_p = cols_of(s_all, p)
+        dots = nt(halves(v_all[blk, :, pair_at(p)]), slopes_p)
+        low = []
+        ds = []
+        for s in range(2):
+            h = 2 * p + s
+            prob = probs[h]
+            low.append(prob.astype(BF16))
+            dot = dots[s * local : (s + 1) * local]
+            ds.append((prob * (dot - deltas[pl.ds(h, 1), :])).astype(BF16))
+        dk = joined(nn(jnp.concatenate(ds, axis=0), queries))
+        dv = joined(nn(jnp.concatenate(low, axis=0), slopes_p))
+        grads_t[1, pair_at(p), :] = dk.T.astype(BF16)
+        grads_t[2, pair_at(p), :] = dv.T.astype(BF16)
+        return carry
+
+    lax.fori_loop(0, pairs, key_side, 0)
+    for o in range(1, n_dp):
+        middle_two = jnp.logical_or(to_dp(o, 1), to_dp(o, 2))
+        pl.when(middle_two)(lambda o=o: col_push(o).start())
+
+    lax.fori_loop(1, 2, gradient, 0)
+    ff_middle(order[0])
+    bias_grad = lax.dot_general(
+        diag[...],
+        onehot[...],
+        (((1,), (1,)), ((), ())),
+        precision=lax.Precision.HIGHEST,
+        preferred_element_type=F32,
+    )
+    small[0:heads, quarter : quarter + n_bucket] = bias_grad[0:heads]
+
+    pl.when(jnp.logical_not(early))(attention_gradient)
+    lax.fori_loop(2, 3, gradient, 0)
+
+    x = tok[...].astype(F32)
+    first_scale = lax.rsqrt(jnp.mean(x * x, axis=-1, keepdims=True) + EPS)
+    key_slope = grads_t[1].astype(F32).T.astype(BF16)
+    value_slope = grads_t[2].astype(F32).T.astype(BF16)
+    first_slope = nt(dq_rows[...], wq[...]) + nt(key_slope, wk[...]) + nt(value_slope, wv[...])
+    small_line(0, jnp.sum(first_slope * x * first_scale, axis=0, keepdims=True))
+
+    def small_blk_push(o):
+        return push(small, small_blk.at[blk], sb_send.at[o], sb_sem.at[o], (blk + o) % n_blk, dp)
+
+    for o in range(1, n_blk):
+        small_blk_push(o).start()
+    small_blk[blk] = small[...]
+    scaled = first_slope * gain1
+    token_slope = (
+        middle[...]
+        + first_scale * scaled
+        - x
+        * (first_scale * first_scale * first_scale)
+        * jnp.mean(scaled * x, axis=-1, keepdims=True)
+    )
+    tokgrad_out[...] = token_slope.T
+
+    ff_middle(order[1])
+    attention_gradient_next()
+    for o in range(1, n_blk):
+        small_blk_push(o).wait_recv()
+    total = small_blk[0]
+    for b in range(1, n_blk):
+        total += small_blk[b]
+    small_dp[dp] = total
+
+    def small_dp_push(o):
+        return push(
+            small_dp.at[dp], small_dp.at[dp], sd_send.at[o], sd_sem.at[o], blk, (dp + o) % n_dp
+        )
+
+    for o in range(1, n_dp):
+        small_dp_push(o).start()
+
+    ff_middle(order[2])
+    mixed_out[...] = mixed_acc[core].T.astype(BF16)
+    for o in range(1, HI):
+        at_hop2(o).wait_recv()
+    total = at_recv[0].astype(F32)
+    for b in range(1, HI):
+        total += at_recv[b].astype(F32)
+    ag[dp] = total.astype(BF16)
+
+    def ag_push(o):
+        return push(ag.at[dp], ag.at[dp], ag_send.at[o], ag_sem.at[o], blk, (dp + o) % n_dp)
+
+    for o in range(1, n_dp):
+        ag_push(o).start()
+    for w in order:
+        ff_last(w)
+
+    for o in range(1, n_dp):
+        small_dp_push(o).wait_recv()
+        ag_push(o).wait_recv()
+    total = small_dp[0]
+    for d in range(1, n_dp):
+        total += small_dp[d]
+    small_out[...] = jnp.zeros_like(small_out)
+    for q in range(4):
+        at = slice(q * quarter, (q + 1) * quarter)
+        small_out[0:1, at] = total[q : q + 1, 0:quarter]
+        small_out[1:2, at] = total[4 + q : 5 + q, 0:quarter]
+    small_out[2 : 2 + heads, 0:n_bucket] = total[0:heads, quarter : quarter + n_bucket]
+    for a in range(4):
+        attn_out[a] = ag[a].astype(F32)
+
+    for ring in (k_ring, v_ring, q_ring, s_ring):
+        ring.drain()
+    for which in range(2):
+        gat_y(which).wait_send()
+        for a in range(2):
+            gat_z(which, a).wait_send()
+            gat_y_far(which, a).wait_send()
+            for b in range(2):
+                gat_core(which, a, b).wait_send()
+
+    @pl.when(lower)
+    def _():
+        row_across().wait_send()
+        row_on().wait_send()
+        row_up().wait_send()
+        row_last(brow).wait_send()
+
+    @pl.when(dp == 2)
+    def _():
+        row_down().wait_send()
+        row_across_last().wait_send()
+
+    for o in range(1, n_dp):
+        col_push(o).wait_send()
+        small_dp_push(o).wait_send()
+        ag_push(o).wait_send()
+    for o in range(1, n_blk):
+        total_push(o).wait_send()
+        delta_push(o).wait_send()
+        small_blk_push(o).wait_send()
+    at_hop1().wait_send()
+    for o in range(1, HI):
+        at_hop2(o).wait_send()
+    for w in order:
+        for hop in ff_hop1(w) + ff_hop2(w):
+            hop.wait_send()
+
+
+def spread_kernel(small, mixed, tokens_gradient, attn, ff_grads, *outs):
+    gain1, gain2, bias, mixed_out, tokens_out = outs[:5]
+    width = gain1.shape[0]
+    gain1[...] = small[0, 0:width]
+    gain2[...] = small[1, 0:width]
+    bias[...] = small[2 : 2 + bias.shape[0], 0 : bias.shape[1]]
+    mixed_out[...] = mixed[...]
+    tokens_out[...] = tokens_gradient[...]
+    for a in range(4):
+        outs[5 + a][...] = attn[a, :, 0:width]
+    for w in range(3):
+        outs[9 + w][...] = ff_grads[w, :, 0:width]
+
+
+def fused(
+    n_blk,
+    n_dp,
+    tokens,
+    lengths,
+    bucket_table,
+    first_gain,
+    position_bias,
+    w_query,
+    w_key,
+    w_value,
+    w_output,
+    second_gain,
+    w_gate,
+    w_up,
+    w_down,
+    cotangent,
+):
+    local, width = tokens.shape[1:]
+    inner = w_query.shape[1]
+    ff = w_gate.shape[1]
+    n_bucket, heads = position_bias.shape
+    keys = n_blk * local
+    cut = ff // (n_blk * n_dp)
+    n_lo = n_blk // HI
+    held = n_lo * (HI // 2) * cut
+    part = inner // n_blk
+    pairs = inner // LANES
+    chunk = 256
+    lanes = -(-width // LANES) * LANES
+    dma, vmem = pltpu.SemaphoreType.DMA, pltpu.VMEM
+    any_spec = pl.BlockSpec(memory_space=pl.ANY)
+    vmem_spec = pl.BlockSpec(memory_space=pltpu.VMEM)
+    smem_spec = pl.BlockSpec(memory_space=pltpu.SMEM)
+    scratch = [
+        vmem((width, local), BF16),
+        vmem((width, local), BF16),
+        vmem((local, width), BF16),
+        vmem((width, inner), BF16),
+        vmem((width, inner), BF16),
+        vmem((width, inner), BF16),
+        vmem((width, inner), BF16),
+        vmem((n_blk, local, inner), BF16),
+        vmem((n_blk, local, inner), BF16),
+        vmem((n_blk, local, inner), BF16),
+        vmem((n_blk, local, inner), BF16),
+        vmem((8, keys), F32),
+        vmem((8, keys), F32),
+        vmem((2 * pairs, local, keys), F32),
+        vmem((local, inner), BF16),
+        vmem((2, 2 * HI, local, lanes), BF16),
+        vmem((3, 4, width, chunk), BF16),
+        vmem((3, held, lanes), BF16),
+        vmem((ff // 2 // chunk, 2 * local, chunk), BF16),
+        vmem((local, width), F32),
+        vmem((2, local, width), F32),
+        vmem((2, local, width), F32),
+        vmem((local, inner), F32),
+        vmem((2, local, lanes), BF16),
+        vmem((2, local, lanes), BF16),
+        vmem((3, n_lo, HI // 2, cut, lanes), BF16),
+        vmem((3, 2, cut, lanes), BF16),
+        vmem((3, cut, lanes), BF16),
+        vmem((n_dp, local, lanes), BF16),
+        vmem((inner, n_dp * local), BF16),
+        vmem((4, inner, local), BF16),
+        vmem((n_lo, HI, part, lanes), BF16),
+        vmem((HI, part, lanes), BF16),
+        vmem((HI, part, lanes), BF16),
+        vmem((n_dp, part, lanes), BF16),
+        vmem((8, lanes // 4 + LANES), F32),
+        vmem((n_blk, 8, lanes // 4 + LANES), F32),
+        vmem((n_dp, 8, lanes // 4 + LANES), F32),
+        vmem((2, heads + heads % 2, 4 * local), F32),
+        vmem((n_bucket, 4 * local), F32),
+        vmem((8, 4 * local), F32),
+        vmem((local, keys + 2 * local), F32),
+        dma((6,)),
+        dma((3, 4)),
+        dma((2,)),
+    ]
+    for shape in (
+        (7,),
+        (7,),
+        (7,),
+        (7,),
+        (n_blk,),
+        (n_blk,),
+        (2, 9),
+        (8,),
+        (n_dp,),
+        (3, 4),
+        (HI,),
+        (n_dp,),
+        (n_blk,),
+        (n_dp,),
+    ):
+        scratch += [dma(shape), dma(shape)]
+    mixed, tokens_gradient, small, attn, ff_grads = pl.pallas_call(
+        functools.partial(layer_kernel, n_blk, n_dp),
+        out_shape=(
+            jax.ShapeDtypeStruct((width, local), BF16),
+            jax.ShapeDtypeStruct((width, local), F32),
+            jax.ShapeDtypeStruct((8, lanes), F32),
+            jax.ShapeDtypeStruct((4, part, lanes), F32),
+            jax.ShapeDtypeStruct((3, cut, lanes), F32),
+        ),
+        in_specs=[smem_spec] + [vmem_spec] * 4 + [any_spec] * 9,
+        out_specs=(vmem_spec,) * 5,
+        scratch_shapes=scratch,
+        compiler_params=pltpu.CompilerParams(
+            collective_id=0, has_side_effects=True, vmem_limit_bytes=64 * 1024 * 1024 - 65536
+        ),
+    )(
+        lengths,
+        bucket_table,
+        first_gain,
+        second_gain,
+        position_bias.T,
+        tokens[0].T,
+        cotangent[0].T,
+        w_query,
+        w_key,
+        w_value,
+        w_output.T,
+        w_gate,
+        w_up,
+        w_down.T,
+    )
+    outs = pl.pallas_call(
+        spread_kernel,
+        out_shape=[
+            jax.ShapeDtypeStruct((width,), F32),
+            jax.ShapeDtypeStruct((width,), F32),
+            jax.ShapeDtypeStruct((heads, n_bucket), F32),
+            jax.ShapeDtypeStruct((width, local), BF16),
+            jax.ShapeDtypeStruct((width, local), F32),
+        ]
+        + [jax.ShapeDtypeStruct((part, width), F32)] * 4
+        + [jax.ShapeDtypeStruct((cut, width), F32)] * 3,
+        in_specs=[vmem_spec] * 5,
+        out_specs=[vmem_spec] * 12,
+    )(small, mixed, tokens_gradient, attn, ff_grads)
+    gain1, gain2, bias, mixed, tokens_gradient, query, key, value, output, gate, up, down = outs
+    return (
+        mixed.T[None],
+        tokens_gradient.T[None],
+        gain1,
+        bias.T,
+        query.T,
+        key.T,
+        value.T,
+        output,
+        gain2,
+        gate.T,
+        up.T,
+        down,
+    )
 
 
 def normalize(values, gain):
@@ -307,8 +1494,18 @@
 
 
 def solution(mesh):
+    n_blk, n_dp = mesh.shape["blk"], mesh.shape["dp"]
+
+    def on_any(*args):
+        local = args[0].shape[1]
+        inner, ff = args[5].shape[1], args[10].shape[1]
+        fits = n_blk * local <= 1024 and n_dp == 4 and n_blk == 2 * HI
+        if fits and ff % (16 * n_blk * n_dp) == 0 and inner % (16 * n_blk) == 0:
+            return fused(n_blk, n_dp, *args)
+        return on_device(*args)
+
     return jax.shard_map(
-        on_device,
+        on_any,
         mesh=mesh,
         in_specs=(
             P("dp", "blk", None),

time: 2670 us -> 135 us (0.05)
  local copies, waits for them, and re-layouts: 1490 us -> 0 us
  waiting for transfers between devices: 801 us -> 0 us
  blocking collectives: 213 us -> 0 us
  Pallas kernels: 0 us -> 134 us
  matrix products: 113 us -> 0 us
    gather x12 -> x0, local copies, waits for them, and re-layouts: 1410 us -> none  [pair_scores(): jnp.take(head_rows, offset, axis=1)]
    reduce_scatter x6 -> x0, waiting for transfers between devices: 569 us -> none  [the longest x1 231 us: on_device(): lax.psum_scatter(up_local, ('blk', 'dp'), scatter_dimension=1, tiled=True)]
    transpose x1 -> x0, waiting for transfers between devices: 232 us -> none  [on_device(): feed_parts[2]]
    all_gather x6 -> x0, blocking collectives: 167 us -> none  [the longest x1 30.1 us: on_device(): lax.all_gather(attention_slope, 'blk', axis=0, tiled=True)]
    pallas_call x0 -> x2, Pallas kernels: none -> 134 us  [the longest x1 130 us: fused(): pl.pallas_call(functools.partial(layer_kernel, n_blk, n_dp), out_shape=(j...]
    dot_general x41 -> x0, matrix products: 113 us -> none  [the longest x6 13.2 us: pair_scores(): jnp.einsum('qhd,khd->hqk', query3, key3, preferred_element_type=f32)]
    psum x1 -> x0, blocking collectives: 45.7 us -> none  [on_device(): lax.psum((first_gain_local, bias_local, second_gain_local), ('blk', 'dp'))]
    unnamed x106 -> x0, local copies, waits for them, and re-layouts: 29.4 us -> none
  transfers between devices with their start and end apart: 8 -> 0, of which waited for: 6 -> 0; matrix products, arithmetic and copies ran while one was open for 22% -> 0% of each run, Pallas kernels for 0% -> 0%
where the time goes in v1:
time: 135 us
  Pallas kernels  134 us (99%)
    pallas_call x1, Pallas kernels, fused(): pl.pallas_call(functools.partial(layer_kernel, n_blk, n_dp), out_shape=(j...  130 us
    pallas_call x1, Pallas kernels, fused(): pl.pallas_call(spread_kernel, out_shape=[jax.ShapeDtypeStruct((width,), F...  4.4 us

profile of v1, /device:TPU:1, one launch (start us, length us, event | category | flops | bytes accessed | tf_op | source)
XLA Modules:
  0.0 134.8 jit_solution(18137688401959764258)
XLA Ops:
  0.6 129.8 %shard_map.229 = (bf16[1472,128]{1,0:T(8,128)(2,1)}, f32[1472,128]{1,0:T(8,128)}, f32[8,1536]{1,0:T(8,128)}, f32[4,48,1536]{2,1,0:T(8,128)}, f32[3,112,1536]{2,1,0:T(8,128)}) custom-call(s32[1,8]{1,0:T(1,128)} %lengths.1, s32[257]{0:T(512)} %bucket_table.1, bf16[1472]{0:T(1024)(128)(2,1)} %first_gain.1, bf16[1472]{0:T(1024)(128)(2,1)} %second_gain.1, ...), custom_call_target="tpu_custom_call" | custom-call | tf_op jit(solution)/shard_map/pallas_call | solution.py:1134
  130.4 4.4 %shard_map.230 = (f32[1472]{0:T(1024)}, f32[1472]{0:T(1024)}, f32[6,32]{1,0:T(8,128)}, bf16[1472,128]{1,0:T(8,128)(2,1)}, f32[1472,128]{1,0:T(8,128)}, /*index=5...) custom-call(f32[8,1536]{1,0:T(8,128)} %get-tuple-element.29.small, ...), custom_call_target="tpu_custom_call" | custom-call | tf_op jit(solution)/shard_map/pallas_call | solution.py:1165

commit v2 on v1

--- a/solution.py
+++ b/solution.py
@@ -604,14 +604,17 @@
     q_ring.step_last()
     lax.fori_loop(n_chunk - 1, n_chunk, feed, 0)
 
-    def swap_push():
-        return push(swap_out, swap_in, swap_sem.at[0], swap_sem.at[1], blk, row_y * 2 + core_other)
+    def swap_push(k):
+        return push(
+            swap_out.at[k], swap_in.at[k], swap_sem.at[k], swap_sem.at[2 + k], blk, other_dp
+        )
 
     swap_out[0] = widen(second_acc[core_other].astype(BF16), lanes)
+    swap_push(0).start()
     swap_out[1] = widen(mixed_acc[core_other].astype(BF16), lanes)
-    swap_push().start()
+    swap_push(1).start()
     gat_forward(0, 0)
-    swap_push().wait_recv()
+    swap_push(0).wait_recv()
 
     mid = middle[...]
     second_scale = lax.rsqrt(jnp.mean(mid * mid, axis=-1, keepdims=True) + EPS)
@@ -634,7 +637,7 @@
         * (second_scale * second_scale * second_scale)
         * jnp.mean(scaled * mid, axis=-1, keepdims=True)
     )
-    mixed_acc[core] = mid + mixed_acc[core] + swap_in[1, :, 0:width].astype(F32)
+    mixed_acc[core] = mid + mixed_acc[core]
     middle[...] = middle_slope
     branch = middle_slope.astype(BF16)
     s_all[blk] = nn(branch, wo[...]).astype(BF16)
@@ -650,7 +653,7 @@
     for o in range(1, n_blk):
         delta_push(o).start()
 
-    swap_push().wait_send()
+    swap_push(0).wait_send()
     brow = swap_out.at[0]
     brow[...] = widen(branch, lanes)
 
@@ -740,23 +743,9 @@
         pl.when(jnp.logical_or(to_dp(o, 0), to_dp(o, last_dp)))(lambda o=o: col_push(o).start())
     pl.when(lower)(lambda: row_up().start())
     s_ring.step_far()
+    gat_across(0, 1)
     lax.fori_loop(1, 2, recompute, 0)
 
-    q_ring.finish()
-    for o in range(1, n_blk):
-        total_push(o).wait_recv()
-
-    def key_weights(p, carry):
-        raw = nt(halves(k_all[blk, :, pair_at(p)]), cols_of(q_all, p))
-        for s in range(2):
-            h = 2 * p + s
-            piece = slice(s * local, (s + 1) * local)
-            probs[h] = jnp.exp(raw[piece] + bias_tile(1, h) - totals[pl.ds(h, 1), :])
-        return carry
-
-    lax.fori_loop(0, pairs, key_weights, 0)
-
-    gat_across(0, 1)
     s_ring.step_last()
     lax.fori_loop(2, HI, recompute, 0)
 
@@ -867,6 +856,21 @@
 
     pl.when(early)(attention_gradient)
     lax.fori_loop(0, 1, gradient, 0)
+
+    q_ring.finish()
+    for o in range(1, n_blk):
+        total_push(o).wait_recv()
+
+    def key_weights(p, carry):
+        raw = nt(halves(k_all[blk, :, pair_at(p)]), cols_of(q_all, p))
+        for s in range(2):
+            h = 2 * p + s
+            piece = slice(s * local, (s + 1) * local)
+            probs[h] = jnp.exp(raw[piece] + bias_tile(1, h) - totals[pl.ds(h, 1), :])
+        return carry
+
+    lax.fori_loop(0, pairs, key_weights, 0)
+
 
     s_ring.finish()
     for o in range(1, n_blk):
@@ -950,7 +954,9 @@
         small_dp_push(o).start()
 
     ff_middle(order[2])
-    mixed_out[...] = mixed_acc[core].T.astype(BF16)
+    swap_push(1).wait_recv()
+    mixed = mixed_acc[core] + swap_in[1, :, 0:width].astype(F32)
+    mixed_out[...] = mixed.T.astype(BF16)
     for o in range(1, HI):
         at_hop2(o).wait_recv()
     total = at_recv[0].astype(F32)
@@ -1011,6 +1017,7 @@
         total_push(o).wait_send()
         delta_push(o).wait_send()
         small_blk_push(o).wait_send()
+    swap_push(1).wait_send()
     at_hop1().wait_send()
     for o in range(1, HI):
         at_hop2(o).wait_send()
@@ -1112,7 +1119,7 @@
         vmem((local, keys + 2 * local), F32),
         dma((6,)),
         dma((3, 4)),
-        dma((2,)),
+        dma((4,)),
     ]
     for shape in (
         (7,),

time: 135 us -> 135 us (level)
  no operation moved by 1% of the time
where the time goes in v2:
time: 135 us
  Pallas kernels  134 us (99%)
    pallas_call x1, Pallas kernels, fused(): pl.pallas_call(functools.partial(layer_kernel, n_blk, n_dp), out_shape=(j...  129 us
    pallas_call x1, Pallas kernels, fused(): pl.pallas_call(spread_kernel, out_shape=[jax.ShapeDtypeStruct((width,), F...  4.4 us

profile of v2, /device:TPU:1, one launch (start us, length us, event | category | flops | bytes accessed | tf_op | source)
XLA Modules:
  0.0 134.5 jit_solution(2462796664717040274)
XLA Ops:
  0.6 129.4 %shard_map.229 = (bf16[1472,128]{1,0:T(8,128)(2,1)}, f32[1472,128]{1,0:T(8,128)}, f32[8,1536]{1,0:T(8,128)}, f32[4,48,1536]{2,1,0:T(8,128)}, f32[3,112,1536]{2,1,0:T(8,128)}) custom-call(s32[1,8]{1,0:T(1,128)} %lengths.1, s32[257]{0:T(512)} %bucket_table.1, bf16[1472]{0:T(1024)(128)(2,1)} %first_gain.1, bf16[1472]{0:T(1024)(128)(2,1)} %second_gain.1, ...), custom_call_target="tpu_custom_call" | custom-call | tf_op jit(solution)/shard_map/pallas_call | solution.py:1141
  130.1 4.4 %shard_map.230 = (f32[1472]{0:T(1024)}, f32[1472]{0:T(1024)}, f32[6,32]{1,0:T(8,128)}, bf16[1472,128]{1,0:T(8,128)(2,1)}, f32[1472,128]{1,0:T(8,128)}, /*index=5...) custom-call(f32[8,1536]{1,0:T(8,128)} %get-tuple-element.29.small, ...), custom_call_target="tpu_custom_call" | custom-call | tf_op jit(solution)/shard_map/pallas_call | solution.py:1172
